TPU v7x, 32 devices: a whole 2x2x4 slice. The times are simulated.
32 devices in a mesh: crop: 4 (over x, core), row: 8 (over z, y).
Axes of the slice: x: 2, y: 2, z: 4, core: 2. Of those that a mesh axis runs over, the one named last changes fastest.
Arguments:
- pair: bfloat16 [64, 16, 128], P(('crop', 'row')), parts along dimension 0, may hold values from -6 to 6
- out_grad: bfloat16 [64, 16, 128], P('crop', 'row'), parts along dimension 0, may hold values from -6 to 6
- w_qkvg: bfloat16 [128, 512], replicated, may hold values from -0.5 to 0.5
- w_out: bfloat16 [128, 128], replicated, may hold values from -0.5 to 0.5
- w_bias: bfloat16 [128, 4], replicated, may hold values from -32 to 32
- gain: float32 [128], replicated, may hold values from 0.1 to 1.9
Outputs:
- d_pair: bfloat16 [64, 16, 128], P(('crop', 'row')), parts along dimension 0
- d_qkvg: float32 [512, 512], P('crop'), parts along dimension 0
- d_wout: float32 [512, 128], P('crop'), parts along dimension 0
- d_wbias: float32 [512, 4], P('crop'), parts along dimension 0
- d_gain: float32 [512], P('crop'), parts along dimension 0
There are 4 independent parts, one for each index of `crop`. A program takes and returns all parts, laid end to end along the dimension named above; an argument that names none is the same for every part. Nothing has to cross between parts.
All inputs are finite; a program needn't handle non-finite values.
Results may differ from a plain program's by a relative error of at most 0.014.
The roundings to bfloat16 on the way count: a program that leaves them out, or rounds other values in their place, can miss the bound.
Values may be sent and summed in bfloat16 or wider, within the bound.
A program may use at most 64 MiB of HBM per device.

v0:
```python
import jax
import jax.numpy as jnp
from jax import lax
from jax.sharding import PartitionSpec as P

DH = 32


EPSILON = 1e-05


def normalize(pair, gain):
    values = pair.astype(jnp.float32)
    center = jnp.mean(values, axis=-1, keepdims=True)
    spread = jnp.mean(jnp.square(values - center), axis=-1, keepdims=True)
    inv_std = lax.rsqrt(spread + EPSILON)
    normed = (values - center) * inv_std
    return ((normed * gain).astype(jnp.bfloat16), normed, inv_std)


def column_grad(tokens, grads, w_qkvg, w_out, bias, scale):
    width = w_out.shape[0]
    heads = bias.shape[0]
    size = width // heads
    count = tokens.shape[0]
    proj = jnp.dot(tokens, w_qkvg, preferred_element_type=jnp.float32)
    queries = proj[:, :width].astype(jnp.bfloat16).reshape(count, heads, size)
    keys = proj[:, width : 2 * width].astype(jnp.bfloat16).reshape(count, heads, size)
    values = proj[:, 2 * width : 3 * width].astype(jnp.bfloat16).reshape(count, heads, size)
    gate = jax.nn.sigmoid(proj[:, 3 * width :]).reshape(count, heads, size)
    scores = jnp.einsum("khd,ihd->hki", keys, queries, preferred_element_type=jnp.float32) * scale
    scores = scores + bias.astype(jnp.float32)
    probs = jax.nn.softmax(scores, axis=1)
    probs_b = probs.astype(jnp.bfloat16)
    attended = jnp.einsum("hki,khd->ihd", probs_b, values, preferred_element_type=jnp.float32)
    mixed = (gate * attended).astype(jnp.bfloat16).reshape(count, width)
    d_mixed = lax.dot_general(
        grads, w_out, (((1,), (1,)), ((), ())), preferred_element_type=jnp.float32
    ).reshape(count, heads, size)
    part_wout = lax.dot_general(
        mixed, grads, (((0,), (0,)), ((), ())), preferred_element_type=jnp.float32
    )
    d_gate = d_mixed * attended * gate * (1.0 - gate)
    d_att = (d_mixed * gate).astype(jnp.bfloat16)
    d_values = jnp.einsum("hki,ihd->khd", probs_b, d_att, preferred_element_type=jnp.float32)
    d_probs = jnp.einsum("ihd,khd->hki", d_att, values, preferred_element_type=jnp.float32)
    delta = jnp.sum(d_att.astype(jnp.float32) * attended, axis=-1)
    d_scores = (probs * (d_probs - delta.T[:, None, :])).astype(jnp.bfloat16)
    d_queries = (
        jnp.einsum("hki,khd->ihd", d_scores, keys, preferred_element_type=jnp.float32) * scale
    )
    d_keys = (
        jnp.einsum("hki,ihd->khd", d_scores, queries, preferred_element_type=jnp.float32) * scale
    )
    d_proj = jnp.concatenate(
        [
            d_queries.reshape(count, width),
            d_keys.reshape(count, width),
            d_values.reshape(count, width),
            d_gate.reshape(count, width),
        ],
        axis=1,
    ).astype(jnp.bfloat16)
    part_qkvg = lax.dot_general(
        tokens, d_proj, (((0,), (0,)), ((), ())), preferred_element_type=jnp.float32
    )
    d_tokens = lax.dot_general(
        d_proj, w_qkvg, (((1,), (1,)), ((), ())), preferred_element_type=jnp.float32
    ).astype(jnp.bfloat16)
    return (d_tokens, d_scores, part_qkvg, part_wout, queries, keys, values, d_att, delta)


def per_device(pair, out_grad, w_qkvg, w_out, w_bias, gain):
    normed_b, normed, inv_std = normalize(pair, gain)
    width = w_out.shape[0]
    heads = w_bias.shape[1]
    scale = DH ** (-0.5)
    columns = lax.all_to_all(normed_b, "row", split_axis=1, concat_axis=0, tiled=True)
    wide_bias = w_bias.astype(jnp.float32)
    local_bias = jnp.einsum(
        "abc,ch->hab", normed_b, w_bias, preferred_element_type=jnp.float32
    ).astype(jnp.bfloat16)
    bias = lax.all_gather(local_bias, "row", axis=1, tiled=True)
    length = bias.shape[1]
    inv_count = 1.0 / length
    inputs = (jnp.swapaxes(columns, 0, 1), jnp.swapaxes(out_grad, 0, 1))

    def step(carry, pieces):
        d_bias, d_qkvg, d_wout = carry
        outs = column_grad(pieces[0], pieces[1], w_qkvg, w_out, bias, scale)
        return ((d_bias + outs[1].astype(jnp.float32), d_qkvg + outs[2], d_wout + outs[3]), outs[0])

    start = (
        jnp.zeros((heads, length, length), jnp.float32),
        jnp.zeros((width, 4 * width), jnp.float32),
        jnp.zeros((width, width), jnp.float32),
    )
    (d_bias, d_qkvg, d_wout), d_cols = lax.scan(step, start, inputs)
    d_att_cols = jnp.swapaxes(d_cols, 0, 1)
    owned = lax.psum_scatter(d_bias, "row", scatter_dimension=1, tiled=True)
    d_att_x = lax.all_to_all(d_att_cols, "row", split_axis=0, concat_axis=1, tiled=True)
    d_bias_x = jnp.einsum("hab,ch->abc", owned, wide_bias, precision=lax.Precision.HIGHEST).astype(
        jnp.bfloat16
    )
    d_wbias = jnp.einsum(
        "abc,hab->ch", normed_b.astype(jnp.float32), owned, precision=lax.Precision.HIGHEST
    )
    d_xn = d_att_x.astype(jnp.float32) + d_bias_x.astype(jnp.float32)
    local_gain = jnp.sum(d_xn * normed, axis=(0, 1))
    scaled = d_xn * gain
    d_pair = (
        inv_std
        * (
            scaled
            - jnp.mean(scaled, axis=-1, keepdims=True)
            - normed * jnp.mean(scaled * normed, axis=-1, keepdims=True)
        )
    ).astype(jnp.bfloat16)
    total_qkvg, total_wout, total_wbias, total_gain = lax.psum(
        (d_qkvg, d_wout, d_wbias, local_gain), "row"
    )
    return (
        d_pair,
        total_qkvg * inv_count,
        total_wout * inv_count,
        total_wbias * inv_count,
        total_gain * inv_count,
    )


def solution(mesh):
    in_specs = (P(("crop", "row"), None, None), P("crop", "row", None), P(), P(), P(), P())
    out_specs = (
        P(("crop", "row"), None, None),
        P("crop", None),
        P("crop", None),
        P("crop", None),
        P("crop"),
    )
    return jax.shard_map(
        per_device, mesh=mesh, in_specs=in_specs, out_specs=out_specs, check_vma=False
    )
```

profile of v0, /device:TPU:0, one launch (start us, length us, event | category | flops | bytes accessed | tf_op | source)
XLA Modules:
  0.0 177.7 jit_solution(12916649451766840287)
XLA Ops:
  7.2 0.8 convert_reduce_fusion
  8.2 0.7 fusion.48
  9.0 0.6 copy.69
  9.6 7.3 %all-to-all-start = ((bf16[2,16,128]{2,0,1:T(2,128)(2,1)}), bf16[2,16,128]{2,0,1:T(2,128)(2,1)S(1)}, u32[]{:S(2)}, u32[]{:S(2)}) async-start(bf16[2,16,128]{2,0,1:T(2,128)(2,1)} %copy.69), calls=%async_computation | async-start | bytes 16384 | tf_op jit(solution)/shard_map/all_to_all | solution.py:78
  17.0 26.6 %all_gather.3 = bf16[4,16,16]{2,0,1:T(4,128)(2,1)S(1)} all-gather(bf16[4,2,16]{2,0,1:T(4,128)(2,1)S(1)} %fusion.41), channel_id=1, replica_groups=mesh['crop'=4,'row'=8] {'row'}, dimensions={1}, use_global_device_ids=true | all-gather | bytes 2304 | tf_op jit(solution)/shard_map/all_gather | solution.py:83
  43.6 0.7 copy-done.7
  44.3 0.6 dynamic-slice
  45.5 6.0 %while.17 = (s32[]{:T(128)}, f32[4,16,16]{2,1,0:T(8,128)S(1)}, f32[128,512]{1,0:T(8,128)S(1)}, f32[128,128]{1,0:T(8,128)S(1)}, bf16[2,16,128]{2,1,0:T(8,128)(2,1...) while((s32[]{:T(128)}, f32[4,16,16]{2,1,0:T(8,128)S(1)}, ...), condition=%wide.region_6.7_spmd.clone, body=%wide.region_2.6_spmd.clone.sunk | while | flops 7966832 | bytes 1377941 | solution.py:98
  46.5 0.3 multiply_reduce_fusion.3
  49.5 0.3 multiply_reduce_fusion.3
  51.6 35.6 %all-reduce = f32[4,16,16]{2,0,1:T(4,128)S(1)} all-reduce(f32[4,16,16]{2,0,1:T(4,128)S(1)} %copy.75), channel_id=2, replica_groups=mesh['crop'=4,'row'=8] {'row'}, use_global_device_ids=true, to_apply=%region_7.8.clone | all-reduce | flops 1024 | bytes 8192
  87.2 0.6 copy.100
  87.8 3.3 %all-to-all-start.1 = ((bf16[16,2,128]{2,1,0:T(2,128)(2,1)}), bf16[16,2,128]{2,1,0:T(2,128)(2,1)S(1)}, u32[]{:S(2)}, u32[]{:S(2)}) async-start(bf16[16,2,128]{2,1,0:T(2,128)(2,1)} %bitcast.69), calls=%async_computation.1 | async-start | bytes 16384 | tf_op jit(solution)/shard_map/all_to_all | solution.py:101
  91.4 0.5 all-reduce.5.cloned.1.call-update
  91.9 5.7 %all-to-all-done.1 = bf16[16,2,128]{2,1,0:T(2,128)(2,1)S(1)} async-done(((bf16[16,2,128]{2,1,0:T(2,128)(2,1)}), bf16[16,2,128]{2,1,0:T(2,128)(2,1)S(1)}, u32[]{:S(2)}, u32[]{:S(2)}) %all-to-all-start.1) | async-done | bytes 8224 | tf_op jit(solution)/shard_map/all_to_all | solution.py:101
  97.6 0.6 copy-done.8
  98.2 0.3 fusion.53
  98.5 17.7 %all-reduce.1 = (f32[128,4]{0,1:T(4,128)S(1)}, f32[128]{0:T(128)S(1)}) all-reduce(f32[128,4]{0,1:T(4,128)S(1)} %convolution_bitcast_fusion.1, f32[128]{0:T(128)S(1)} %get-tuple-element.127), channel_id=1, replica_groups=mesh['crop'=4,'row'=8] {'row'}, use_global_device_ids=true, to_apply=%region_12.13 | all-reduce | flops 640 | bytes 5120 | tf_op jit(solution)/shard_map/psum | solution.py:119
  116.2 0.6 broadcast_multiply_fusion.2
  116.8 0.5 broadcast_multiply_fusion.6
  117.3 0.7 fusion.52
  118.0 50.5 %all-reduce.5.cloned.1.call-done = (f32[128,512]{1,0:T(8,128)}, f32[128,128]{1,0:T(8,128)}) async-done(((f32[128,512]{1,0:T(8,128)}, f32[128,128]{1,0:T(8,128)}), (f32[128,512]{1,0:T(8,128)}, f32[128,128]{1,0:T(8,128)})) %all-reduce.5.cloned.1.call-update) | async-done | bytes 327696 | tf_op jit(solution)/shard_map/psum | solution.py:119
  168.5 1.7 broadcast_multiply_fusion
  170.3 0.6 broadcast_multiply_fusion.1
  (97 shorter events, 5.8 us)
Async XLA Ops:
  7.2 9.7 %copy-start = (bf16[128,4]{0,1:T(4,128)(2,1)S(1)}, bf16[128,4]{0,1:T(4,128)(2,1)}, u32[]{:S(2)}) copy-start(bf16[128,4]{0,1:T(4,128)(2,1)} %param.12) | copy-start | bytes 3076
  7.2 0.9 copy-start.5
  7.2 38.3 %copy-start.1 = (bf16[128,512]{1,0:T(8,128)(2,1)S(1)}, bf16[128,512]{1,0:T(8,128)(2,1)}, u32[]{:S(2)}) copy-start(bf16[128,512]{1,0:T(8,128)(2,1)} %param.10) | copy-start | bytes 393220
  9.6 35.9 %all-to-all-start = ((bf16[2,16,128]{2,0,1:T(2,128)(2,1)}), bf16[2,16,128]{2,0,1:T(2,128)(2,1)S(1)}, u32[]{:S(2)}, u32[]{:S(2)}) async-start(bf16[2,16,128]{2,0,1:T(2,128)(2,1)} %copy.69), calls=%async_computation | async-start | bytes 16384 | tf_op jit(solution)/shard_map/all_to_all | solution.py:78
  43.5 0.7 copy-start.7
  43.6 0.7 copy-start.9
  44.2 1.3 copy-start.4
  51.6 35.6 %copy-start.3 = (f32[128,128]{1,0:T(8,128)}, f32[128,128]{1,0:T(8,128)S(1)}, u32[]{:S(2)}) copy-start(f32[128,128]{1,0:T(8,128)S(1)} %get-tuple-element.63) | copy-start | bytes 196612
  51.6 39.8 %copy-start.2 = (f32[128,512]{1,0:T(8,128)}, f32[128,512]{1,0:T(8,128)S(1)}, u32[]{:S(2)}) copy-start(f32[128,512]{1,0:T(8,128)S(1)} %get-tuple-element.62) | copy-start | bytes 786436
  87.8 9.8 %all-to-all-start.1 = ((bf16[16,2,128]{2,1,0:T(2,128)(2,1)}), bf16[16,2,128]{2,1,0:T(2,128)(2,1)S(1)}, u32[]{:S(2)}, u32[]{:S(2)}) async-start(bf16[16,2,128]{2,1,0:T(2,128)(2,1)} %bitcast.69), calls=%async_computation.1 | async-start | bytes 16384 | tf_op jit(solution)/shard_map/all_to_all | solution.py:101
  91.1 77.4 %all-reduce.5.cloned.1.call-start = ((), (), s32[]{:S(2)}) async-start(), calls=%async_computation.2 | async-start | bytes 655360 | tf_op jit(solution)/shard_map/psum | solution.py:119
  97.6 0.7 copy-start.8
  168.5 1.7 copy-start.6
Sparse Core Ops, SparseCore 0:
  95.9 72.5 all-reduce.4
where the time goes:
time: 178 us
  blocking collectives  79.8 us (45%)
  waiting for transfers between devices  56.8 us (32%)
  between operations  14.8 us (8%)
  starting transfers between devices  10.7 us (6%)
  other arithmetic  6.17 us (3%)
  local copies, waits for them, and re-layouts  4.97 us (3%)
  matrix products  4.37 us (2%)
    psum x1, waiting for transfers between devices, per_device(): lax.psum((d_qkvg, d_wout, d_wbias, local_gain), 'row')  50.5 us
    unnamed x1, blocking collectives  35.6 us
    all_gather x1, blocking collectives, per_device(): bias = lax.all_gather(local_bias, 'row', axis=1, tiled=True)  26.6 us
    psum x1, blocking collectives, per_device(): lax.psum((d_qkvg, d_wout, d_wbias, local_gain), 'row')  17.7 us
    all_to_all x1, starting transfers between devices, per_device(): lax.all_to_all(normed_b, 'row', split_axis=1, concat_axis=0, tiled=True)  7.28 us
    all_to_all x1, waiting for transfers between devices, per_device(): lax.all_to_all(d_att_cols, 'row', split_axis=0, concat_axis=1, tiled=True)  5.71 us
  transfers between devices with their start and end apart: 3, of which 2 were waited for; matrix products, arithmetic and copies ran while one was open for 2% of the time, Pallas kernels for 0%

commit v1 on v0

--- a/solution.py
+++ b/solution.py
@@ -1,6 +1,10 @@
+import functools
+
 import jax
 import jax.numpy as jnp
 from jax import lax
+from jax.experimental import pallas as pl
+from jax.experimental.pallas import tpu as pltpu
 from jax.sharding import PartitionSpec as P
 
 DH = 32
@@ -70,7 +74,7 @@
     return (d_tokens, d_scores, part_qkvg, part_wout, queries, keys, values, d_att, delta)
 
 
-def per_device(pair, out_grad, w_qkvg, w_out, w_bias, gain):
+def sharded_plan(pair, out_grad, w_qkvg, w_out, w_bias, gain):
     normed_b, normed, inv_std = normalize(pair, gain)
     width = w_out.shape[0]
     heads = w_bias.shape[1]
@@ -128,6 +132,261 @@
     )
 
 
+BLOCK = 128
+MASKED = -1e30
+BF16 = jnp.bfloat16
+F32 = jnp.float32
+
+
+def mm(a, b, dims=(1, 0)):
+    return lax.dot_general(
+        a, b, (((dims[0],), (dims[1],)), ((), ())), preferred_element_type=F32
+    )
+
+
+def log2(value):
+    return value.bit_length() - 1
+
+
+def exchange(n, pair_ref, grad_ref, pairs_ref, grads_ref, send_sems, recv_sems, local_sems):
+    me = lax.axis_index("row")
+    barrier = pltpu.get_barrier_semaphore()
+    for offset in range(1, n):
+        pl.semaphore_signal(
+            barrier,
+            inc=1,
+            device_id={"row": lax.rem(me + offset, n)},
+            device_id_type=pl.DeviceIdType.MESH,
+        )
+    own = [
+        pltpu.make_async_copy(pair_ref, pairs_ref.at[me], local_sems.at[0]),
+        pltpu.make_async_copy(grad_ref, grads_ref.at[me], local_sems.at[1]),
+    ]
+    for copy in own:
+        copy.start()
+    pl.semaphore_wait(barrier, n - 1)
+    copies = []
+    for kind, (src, dst) in enumerate(((pair_ref, pairs_ref), (grad_ref, grads_ref))):
+        for offset in range(1, n):
+            copy = pltpu.make_async_remote_copy(
+                src_ref=src,
+                dst_ref=dst.at[me],
+                send_sem=send_sems.at[kind, offset],
+                recv_sem=recv_sems.at[kind, offset],
+                device_id={"row": lax.rem(me + offset, n)},
+                device_id_type=pl.DeviceIdType.MESH,
+            )
+            copy.start()
+            copies.append(copy)
+    for copy in own + copies:
+        copy.wait()
+
+
+def whole_crop(
+    local,
+    pairs_ref,
+    grads_ref,
+    w_qkvg_ref,
+    w_out_ref,
+    w_bias_ref,
+    gain_ref,
+    d_pair_ref,
+    d_qkvg_ref,
+    d_wout_ref,
+    d_wbias_ref,
+    d_gain_ref,
+    d_xn_ref,
+    normed_ref,
+    inv_ref,
+):
+    me = lax.axis_index("row")
+    chunk = pairs_ref.shape[1]
+    width = pairs_ref.shape[2]
+    heads = w_bias_ref.shape[0]
+    size = width // heads
+    length = chunk // local
+    cells = length * length
+    scale = size ** (-0.5)
+    inv_count = 1.0 / length
+    s_local, s_length, s_chunk = log2(local), log2(length), log2(chunk)
+
+    def iota(shape, axis):
+        return lax.broadcasted_iota(jnp.int32, shape, axis)
+
+    def row_of(position):
+        return (position & (chunk - 1)) >> s_local
+
+    g, r = iota((cells, cells), 0), iota((cells, cells), 1)
+    cell = (row_of(g) << s_length) + ((g >> s_chunk) << s_local) + (g & (local - 1))
+    permute = (cell == r).astype(F32).astype(BF16)
+    p, q = iota((BLOCK, BLOCK), 0), iota((BLOCK, BLOCK), 1)
+    same_column = ((p >> s_chunk) == (q >> s_chunk)) & (((p ^ q) & (local - 1)) == 0)
+    p, r = iota((BLOCK, cells), 0), iota((BLOCK, cells), 1)
+    spread_key = (row_of(p) == (r >> s_length)).astype(F32).astype(BF16)
+    r, p = iota((cells, BLOCK), 0), iota((cells, BLOCK), 1)
+    pick_key = (row_of(p) == (r >> s_length)).astype(F32).astype(BF16)
+    pick_query = row_of(p) == (r & (length - 1))
+    lane_head = iota((BLOCK, width), 1) >> log2(size)
+
+    def per_head(block):
+        zero = jnp.zeros_like(block)
+        return jnp.concatenate([jnp.where(lane_head == h, block, zero) for h in range(heads)], 0)
+
+    def own_head(stacked):
+        out = stacked[:BLOCK]
+        for h in range(1, heads):
+            out = jnp.where(lane_head == h, stacked[h * BLOCK : (h + 1) * BLOCK], out)
+        return out
+
+    w_bias = w_bias_ref[...]
+    w_bias_rows = jnp.concatenate(
+        [jnp.broadcast_to(w_bias[h : h + 1], (BLOCK, width)) for h in range(heads)], 0
+    ).astype(BF16)
+    w_qkvg = w_qkvg_ref[...]
+    w_out = w_out_ref[...]
+    gain = gain_ref[...]
+
+    values = pairs_ref[...].reshape(cells, width).astype(F32)
+    center = jnp.mean(values, axis=-1, keepdims=True)
+    spread = jnp.mean(jnp.square(values - center), axis=-1, keepdims=True)
+    inv_std = lax.rsqrt(spread + EPSILON)
+    normed = (values - center) * inv_std
+    xn = (normed * gain).astype(BF16)
+    normed_ref[...] = normed
+    inv_ref[...] = jnp.broadcast_to(inv_std, (cells, width))
+
+    tokens = mm(permute, xn).astype(BF16)
+    proj = mm(tokens, w_qkvg)
+    bias_cells = mm(xn, w_bias_rows, (1, 1))
+    bias = mm(
+        spread_key,
+        jnp.concatenate(
+            [
+                jnp.where(pick_query, bias_cells[:, h * BLOCK : (h + 1) * BLOCK], 0.0)
+                for h in range(heads)
+            ],
+            1,
+        ).astype(BF16),
+    )
+    bias = jnp.concatenate(
+        [
+            jnp.where(same_column, bias[:, h * BLOCK : (h + 1) * BLOCK], MASKED)
+            for h in range(heads)
+        ],
+        0,
+    )
+    grads = grads_ref[...].reshape(cells, width)
+    d_mixed_all = mm(grads, w_out, (1, 1))
+
+    mixed_parts, d_proj_parts = [], []
+    d_bias_x = jnp.zeros((cells, width), F32)
+    d_wbias = jnp.zeros((heads * BLOCK, width), F32)
+    for start in range(0, cells, BLOCK):
+        rows = slice(start, start + BLOCK)
+        queries = proj[rows, :width].astype(BF16)
+        keys = per_head(proj[rows, width : 2 * width]).astype(BF16)
+        vals = per_head(proj[rows, 2 * width : 3 * width]).astype(BF16)
+        gate = jax.nn.sigmoid(proj[rows, 3 * width :])
+        scores = mm(keys, queries, (1, 1)) * scale + bias
+        scores = scores.reshape(heads, BLOCK, BLOCK)
+        top = jnp.max(scores, axis=1, keepdims=True)
+        weights = jnp.exp(scores - top)
+        probs = weights / jnp.sum(weights, axis=1, keepdims=True)
+        probs_b = probs.astype(BF16)
+        flat_b = probs_b.reshape(heads * BLOCK, BLOCK)
+        attended = mm(flat_b, vals, (0, 0))
+        d_mixed = d_mixed_all[rows]
+        mixed_parts.append((gate * attended).astype(BF16))
+        d_gate = d_mixed * attended * gate * (1.0 - gate)
+        d_att = (d_mixed * gate).astype(BF16)
+        d_values = own_head(mm(flat_b, d_att))
+        d_probs = mm(vals, d_att, (1, 1)).reshape(heads, BLOCK, BLOCK)
+        delta = jnp.sum(probs_b.astype(F32) * d_probs, axis=1, keepdims=True)
+        d_scores = (probs * (d_probs - delta)).astype(BF16)
+        flat_d = d_scores.reshape(heads * BLOCK, BLOCK)
+        d_queries = mm(flat_d, keys, (0, 0)) * scale
+        d_keys = own_head(mm(flat_d, queries)) * scale
+        d_proj_parts.append(
+            jnp.concatenate([d_queries, d_keys, d_values, d_gate], 1).astype(BF16)
+        )
+        terms = mm(pick_key, jnp.concatenate([d_scores[h] for h in range(heads)], 1))
+        terms = jnp.concatenate(
+            [
+                jnp.where(pick_query, terms[:, h * BLOCK : (h + 1) * BLOCK], 0.0)
+                for h in range(heads)
+            ],
+            1,
+        ).astype(BF16)
+        d_bias_x = d_bias_x + mm(terms, w_bias_rows)
+        d_wbias = d_wbias + mm(terms, xn, (0, 0))
+
+    d_proj = jnp.concatenate(d_proj_parts, 0)
+    mixed = jnp.concatenate(mixed_parts, 0)
+    d_qkvg_ref[...] = mm(tokens, d_proj, (0, 0)) * inv_count
+    d_wout_ref[...] = mm(mixed, grads, (0, 0)) * inv_count
+    d_wbias_ref[...] = jnp.sum(d_wbias.reshape(heads, BLOCK, width), axis=1) * inv_count
+    d_tokens = mm(d_proj, w_qkvg, (1, 1)).astype(BF16)
+    d_xn = mm(permute, d_tokens, (0, 0)) + d_bias_x.astype(BF16).astype(F32)
+    d_gain_ref[...] = jnp.sum(d_xn * normed, axis=0, keepdims=True) * inv_count
+    d_xn_ref[...] = d_xn
+
+    own = pl.ds(pl.multiple_of(me * chunk, chunk), chunk)
+    normed = normed_ref[own, :]
+    scaled = d_xn_ref[own, :] * gain
+    d_pair = inv_ref[own, :] * (
+        scaled
+        - jnp.mean(scaled, axis=-1, keepdims=True)
+        - normed * jnp.mean(scaled * normed, axis=-1, keepdims=True)
+    )
+    d_pair_ref[...] = d_pair.astype(BF16).reshape(d_pair_ref.shape)
+
+
+def gathered_plan(n, pair, out_grad, w_qkvg, w_out, w_bias, gain):
+    local, length, width = pair.shape
+    heads = w_bias.shape[1]
+    cells = length * length
+    chunk = local * length
+    vmem = pl.BlockSpec(memory_space=pltpu.VMEM)
+    hbm = pl.BlockSpec(memory_space=pl.ANY)
+    pairs, grads = pl.pallas_call(
+        functools.partial(exchange, n),
+        out_shape=[jax.ShapeDtypeStruct((n, chunk, width), BF16)] * 2,
+        in_specs=[hbm] * 2,
+        out_specs=[vmem] * 2,
+        scratch_shapes=[
+            pltpu.SemaphoreType.DMA((2, n)),
+            pltpu.SemaphoreType.DMA((2, n)),
+            pltpu.SemaphoreType.DMA((2,)),
+        ],
+        compiler_params=pltpu.CompilerParams(collective_id=0, has_side_effects=True),
+    )(pair.reshape(chunk, width), out_grad.reshape(chunk, width))
+    d_pair, d_qkvg, d_wout, d_wbias, d_gain = pl.pallas_call(
+        functools.partial(whole_crop, local),
+        out_shape=[
+            jax.ShapeDtypeStruct(pair.shape, BF16),
+            jax.ShapeDtypeStruct(w_qkvg.shape, F32),
+            jax.ShapeDtypeStruct(w_out.shape, F32),
+            jax.ShapeDtypeStruct((heads, width), F32),
+            jax.ShapeDtypeStruct((1, width), F32),
+        ],
+        in_specs=[vmem] * 6,
+        out_specs=[vmem] * 5,
+        scratch_shapes=[pltpu.VMEM((cells, width), F32)] * 3,
+        compiler_params=pltpu.CompilerParams(vmem_limit_bytes=32 * 1024 * 1024),
+    )(pairs, grads, w_qkvg, w_out, w_bias.T, gain.reshape(1, width))
+    return (d_pair, d_qkvg, d_wout, d_wbias.T, d_gain.reshape(width))
+
+
+def per_device(n, pair, out_grad, w_qkvg, w_out, w_bias, gain):
+    local, length, width = pair.shape
+    chunk = local * length
+    powers = all(size & (size - 1) == 0 for size in (local, length, width, w_bias.shape[1]))
+    fits = n > 1 and width == BLOCK and chunk % 16 == 0 and BLOCK % chunk == 0
+    if powers and fits and length * length % BLOCK == 0 and length <= 32:
+        return gathered_plan(n, pair, out_grad, w_qkvg, w_out, w_bias, gain)
+    return sharded_plan(pair, out_grad, w_qkvg, w_out, w_bias, gain)
+
+
 def solution(mesh):
     in_specs = (P(("crop", "row"), None, None), P("crop", "row", None), P(), P(), P(), P())
     out_specs = (
@@ -138,5 +397,7 @@
         P("crop"),
     )
     return jax.shard_map(
-        per_device, mesh=mesh, in_specs=in_specs, out_specs=out_specs, check_vma=False
-    )
+        functools.partial(per_device, mesh.shape["row"]),
+        mesh=mesh,
+        in_specs=in_specs, out_specs=out_specs, check_vma=False
+    )

time: 178 us -> 19.3 us (0.11)
  blocking collectives: 79.8 us -> 0 us
  waiting for transfers between devices: 56.8 us -> 0 us
  Pallas kernels: 0 us -> 14.4 us
  between operations: 14.8 us -> 0.66 us
  starting transfers between devices: 10.7 us -> 0 us
  other arithmetic: 6.17 us -> 0 us
  matrix products: 4.37 us -> 0 us
    psum x1 -> x0, waiting for transfers between devices: 50.5 us -> none  [per_device(): lax.psum((d_qkvg, d_wout, d_wbias, local_gain), 'row')]
    unnamed x1 -> x0, blocking collectives: 35.6 us -> none
    all_gather x1 -> x0, blocking collectives: 26.6 us -> none  [per_device(): bias = lax.all_gather(local_bias, 'row', axis=1, tiled=True)]
    psum x1 -> x0, blocking collectives: 17.7 us -> none  [per_device(): lax.psum((d_qkvg, d_wout, d_wbias, local_gain), 'row')]
    pallas_call x0 -> x2, Pallas kernels: none -> 14.4 us  [the longest x1 10.8 us: gathered_plan(): pl.pallas_call(functools.partial(exchange, n), out_shape=[jax.ShapeDtypeS...]
    all_to_all x2 -> x0, starting transfers between devices: 10.6 us -> none  [the longest x1 7.28 us: per_device(): lax.all_to_all(normed_b, 'row', split_axis=1, concat_axis=0, tiled=True)]
    all_to_all x2 -> x0, waiting for transfers between devices: 5.72 us -> none  [the longest x1 5.71 us: per_device(): lax.all_to_all(d_att_cols, 'row', split_axis=0, concat_axis=1, tiled=True)]
    dot_general x25 -> x0, matrix products: 4.37 us -> none  [the longest x2 0.63 us: column_grad(): jnp.einsum('hki,khd->ihd', probs_b, values, preferred_element_type=jnp.fl...]
  transfers between devices with their start and end apart: 3 -> 0, of which waited for: 2 -> 0; matrix products, arithmetic and copies ran while one was open for 2% -> 0% of each run, Pallas kernels for 0% -> 0%
where the time goes in v1:
time: 19.3 us; the launch traced here: 19 us
  Pallas kernels  14.4 us (75%)
  local copies, waits for them, and re-layouts  4.01 us (21%)
  between operations  0.66 us (3%)
    pallas_call x1, Pallas kernels, gathered_plan(): pl.pallas_call(functools.partial(exchange, n), out_shape=[jax.ShapeDtypeS...  10.8 us
    unnamed x12, local copies, waits for them, and re-layouts  4.01 us
    pallas_call x1, Pallas kernels, gathered_plan(): pl.pallas_call(functools.partial(whole_crop, local), out_shape=[jax.Shape...  3.55 us

profile of v1, /device:TPU:0, one launch (start us, length us, event | category | flops | bytes accessed | tf_op | source)
XLA Modules:
  0.0 19.0 jit_solution(7043586281518857800)
XLA Ops:
  0.6 10.8 %shard_map.101 = (bf16[8,32,128]{2,1,0:T(8,128)(2,1)}, bf16[8,32,128]{2,1,0:T(8,128)(2,1)}) custom-call(bf16[32,128]{1,0:T(8,128)(2,1)} %bitcast.8, bf16[32,128]{1,0:T(8,128)(2,1)} %bitcast.9), custom_call_target="tpu_custom_call" | custom-call | tf_op jit(solution)/shard_map/pallas_call | solution.py:351
  11.5 0.0 copy-start.4
  11.5 0.0 copy-start.5
  11.5 0.7 %copy-done.4 = bf16[128,4]{0,1:T(4,128)(2,1)S(1)} copy-done((bf16[128,4]{0,1:T(4,128)(2,1)S(1)}, bf16[128,4]{0,1:T(4,128)(2,1)}, u32[]{:S(2)}) %copy-start.4) | copy-done | bytes 1048
  12.1 0.0 copy-done.5
  12.1 0.0 copy-start
  12.1 0.9 %copy-done = bf16[128,512]{1,0:T(8,128)(2,1)S(1)} copy-done((bf16[128,512]{1,0:T(8,128)(2,1)S(1)}, bf16[128,512]{1,0:T(8,128)(2,1)}, u32[]{:S(2)}) %copy-start) | copy-done | bytes 131096
  13.1 0.0 copy-start.1
  13.1 0.8 %copy-done.1 = bf16[8,32,128]{2,1,0:T(8,128)(2,1)S(1)} copy-done((bf16[8,32,128]{2,1,0:T(8,128)(2,1)S(1)}, bf16[8,32,128]{2,1,0:T(8,128)(2,1)}, u32[]{:S(2)}) %copy-start.1) | copy-done | bytes 65560
  13.9 0.0 copy-start.2
  13.9 0.8 %copy-done.2 = bf16[8,32,128]{2,1,0:T(8,128)(2,1)S(1)} copy-done((bf16[8,32,128]{2,1,0:T(8,128)(2,1)S(1)}, bf16[8,32,128]{2,1,0:T(8,128)(2,1)}, u32[]{:S(2)}) %copy-start.2) | copy-done | bytes 65560
  14.7 0.0 copy-start.3
  14.7 0.8 %copy-done.3 = bf16[128,128]{1,0:T(8,128)(2,1)S(1)} copy-done((bf16[128,128]{1,0:T(8,128)(2,1)S(1)}, bf16[128,128]{1,0:T(8,128)(2,1)}, u32[]{:S(2)}) %copy-start.3) | copy-done | bytes 32792
  15.5 3.5 %shard_map.102 = (bf16[2,16,128]{2,1,0:T(8,128)(2,1)}, f32[128,512]{1,0:T(8,128)}, f32[128,128]{1,0:T(8,128)}, f32[4,128]{1,0:T(4,128)}, f32[1,128]{1,0:T(1,128)}) custom-call(bf16[8,32,128]{2,1,0:T(8,128)(2,1)S(1)} %copy-done.1, bf16[8,32,128]{2,1,0:T(8,128)(2,1)S(1)} %copy-done.2, bf16[128,512]{1,0:T(8,128)(2,1)S(1)} %copy-done, ...), custom_call_target="tpu_custom_call" | custom-call | tf_op jit(solution)/shard_map/pallas_call | solution.py:363
Async XLA Ops:
  11.5 0.7 %copy-start.4 = (bf16[128,4]{0,1:T(4,128)(2,1)S(1)}, bf16[128,4]{0,1:T(4,128)(2,1)}, u32[]{:S(2)}) copy-start(bf16[128,4]{0,1:T(4,128)(2,1)} %param.10) | copy-start | bytes 3076
  11.5 0.7 %copy-start.5 = (f32[128]{0:T(128)S(1)}, f32[128]{0:T(128)}, u32[]{:S(2)}) copy-start(f32[128]{0:T(128)} %param.11) | copy-start | bytes 1540
  12.1 0.9 %copy-start = (bf16[128,512]{1,0:T(8,128)(2,1)S(1)}, bf16[128,512]{1,0:T(8,128)(2,1)}, u32[]{:S(2)}) copy-start(bf16[128,512]{1,0:T(8,128)(2,1)} %w_qkvg_ref.1) | copy-start | bytes 393220
  13.1 0.8 %copy-start.1 = (bf16[8,32,128]{2,1,0:T(8,128)(2,1)S(1)}, bf16[8,32,128]{2,1,0:T(8,128)(2,1)}, u32[]{:S(2)}) copy-start(bf16[8,32,128]{2,1,0:T(8,128)(2,1)} %get-tuple-element.12.pairs_ref) | copy-start | bytes 196612
  13.9 0.8 %copy-start.2 = (bf16[8,32,128]{2,1,0:T(8,128)(2,1)S(1)}, bf16[8,32,128]{2,1,0:T(8,128)(2,1)}, u32[]{:S(2)}) copy-start(bf16[8,32,128]{2,1,0:T(8,128)(2,1)} %get-tuple-element.13.grads_ref) | copy-start | bytes 196612
  14.7 0.8 %copy-start.3 = (bf16[128,128]{1,0:T(8,128)(2,1)S(1)}, bf16[128,128]{1,0:T(8,128)(2,1)}, u32[]{:S(2)}) copy-start(bf16[128,128]{1,0:T(8,128)(2,1)} %w_out_ref.1) | copy-start | bytes 98308

commit v2 on v1

--- a/solution.py
+++ b/solution.py
@@ -133,6 +133,7 @@
 
 
 BLOCK = 128
+VMEM_LIMIT = 60 * 1024 * 1024
 MASKED = -1e30
 BF16 = jnp.bfloat16
 F32 = jnp.float32
@@ -148,7 +149,33 @@
     return value.bit_length() - 1
 
 
-def exchange(n, pair_ref, grad_ref, pairs_ref, grads_ref, send_sems, recv_sems, local_sems):
+def whole_crop(
+    n,
+    local,
+    pair_hbm,
+    grad_hbm,
+    w_qkvg_hbm,
+    w_out_hbm,
+    w_bias_hbm,
+    gain_hbm,
+    d_pair_ref,
+    d_qkvg_ref,
+    d_wout_ref,
+    d_wbias_ref,
+    d_gain_ref,
+    pairs_ref,
+    grads_ref,
+    w_qkvg_ref,
+    w_out_ref,
+    w_bias_ref,
+    gain_ref,
+    d_xn_ref,
+    normed_ref,
+    inv_ref,
+    send_sems,
+    recv_sems,
+    local_sems,
+):
     me = lax.axis_index("row")
     barrier = pltpu.get_barrier_semaphore()
     for offset in range(1, n):
@@ -158,15 +185,24 @@
             device_id={"row": lax.rem(me + offset, n)},
             device_id_type=pl.DeviceIdType.MESH,
         )
-    own = [
-        pltpu.make_async_copy(pair_ref, pairs_ref.at[me], local_sems.at[0]),
-        pltpu.make_async_copy(grad_ref, grads_ref.at[me], local_sems.at[1]),
+    staged = [
+        pltpu.make_async_copy(src, dst, local_sems.at[index])
+        for index, (src, dst) in enumerate(
+            (
+                (pair_hbm, pairs_ref.at[me]),
+                (gain_hbm, gain_ref),
+                (w_qkvg_hbm, w_qkvg_ref),
+                (w_bias_hbm, w_bias_ref),
+                (grad_hbm, grads_ref.at[me]),
+                (w_out_hbm, w_out_ref),
+            )
+        )
     ]
-    for copy in own:
+    for copy in staged:
         copy.start()
     pl.semaphore_wait(barrier, n - 1)
-    copies = []
-    for kind, (src, dst) in enumerate(((pair_ref, pairs_ref), (grad_ref, grads_ref))):
+    sent = []
+    for kind, (src, dst) in enumerate(((pair_hbm, pairs_ref), (grad_hbm, grads_ref))):
         for offset in range(1, n):
             copy = pltpu.make_async_remote_copy(
                 src_ref=src,
@@ -177,29 +213,8 @@
                 device_id_type=pl.DeviceIdType.MESH,
             )
             copy.start()
-            copies.append(copy)
-    for copy in own + copies:
-        copy.wait()
-
-
-def whole_crop(
-    local,
-    pairs_ref,
-    grads_ref,
-    w_qkvg_ref,
-    w_out_ref,
-    w_bias_ref,
-    gain_ref,
-    d_pair_ref,
-    d_qkvg_ref,
-    d_wout_ref,
-    d_wbias_ref,
-    d_gain_ref,
-    d_xn_ref,
-    normed_ref,
-    inv_ref,
-):
-    me = lax.axis_index("row")
+            sent.append(copy)
+
     chunk = pairs_ref.shape[1]
     width = pairs_ref.shape[2]
     heads = w_bias_ref.shape[0]
@@ -238,12 +253,16 @@
             out = jnp.where(lane_head == h, stacked[h * BLOCK : (h + 1) * BLOCK], out)
         return out
 
+    for copy in staged[:4]:
+        copy.wait()
+    for copy in sent[: n - 1]:
+        copy.wait_recv()
+
     w_bias = w_bias_ref[...]
     w_bias_rows = jnp.concatenate(
         [jnp.broadcast_to(w_bias[h : h + 1], (BLOCK, width)) for h in range(heads)], 0
     ).astype(BF16)
     w_qkvg = w_qkvg_ref[...]
-    w_out = w_out_ref[...]
     gain = gain_ref[...]
 
     values = pairs_ref[...].reshape(cells, width).astype(F32)
@@ -275,12 +294,7 @@
         ],
         0,
     )
-    grads = grads_ref[...].reshape(cells, width)
-    d_mixed_all = mm(grads, w_out, (1, 1))
-
-    mixed_parts, d_proj_parts = [], []
-    d_bias_x = jnp.zeros((cells, width), F32)
-    d_wbias = jnp.zeros((heads * BLOCK, width), F32)
+    forward = []
     for start in range(0, cells, BLOCK):
         rows = slice(start, start + BLOCK)
         queries = proj[rows, :width].astype(BF16)
@@ -295,6 +309,22 @@
         probs_b = probs.astype(BF16)
         flat_b = probs_b.reshape(heads * BLOCK, BLOCK)
         attended = mm(flat_b, vals, (0, 0))
+        forward.append((queries, keys, vals, gate, probs, probs_b, attended))
+
+    for copy in staged[4:]:
+        copy.wait()
+    for copy in sent[n - 1 :]:
+        copy.wait_recv()
+    grads = grads_ref[...].reshape(cells, width)
+    d_mixed_all = mm(grads, w_out_ref[...], (1, 1))
+
+    mixed_parts, d_proj_parts = [], []
+    d_bias_x = jnp.zeros((cells, width), F32)
+    d_wbias = jnp.zeros((heads * BLOCK, width), F32)
+    for start in range(0, cells, BLOCK):
+        queries, keys, vals, gate, probs, probs_b, attended = forward[start // BLOCK]
+        rows = slice(start, start + BLOCK)
+        flat_b = probs_b.reshape(heads * BLOCK, BLOCK)
         d_mixed = d_mixed_all[rows]
         mixed_parts.append((gate * attended).astype(BF16))
         d_gate = d_mixed * attended * gate * (1.0 - gate)
@@ -339,6 +369,19 @@
         - normed * jnp.mean(scaled * normed, axis=-1, keepdims=True)
     )
     d_pair_ref[...] = d_pair.astype(BF16).reshape(d_pair_ref.shape)
+    for copy in sent:
+        copy.wait_send()
+
+
+def deliver(count, *refs):
+    copies = [
+        pltpu.make_async_copy(refs[index], refs[count + index], refs[-1].at[index])
+        for index in range(count)
+    ]
+    for copy in copies:
+        copy.start()
+    for copy in copies:
+        copy.wait()
 
 
 def gathered_plan(n, pair, out_grad, w_qkvg, w_out, w_bias, gain):
@@ -347,33 +390,54 @@
     cells = length * length
     chunk = local * length
     vmem = pl.BlockSpec(memory_space=pltpu.VMEM)
-    hbm = pl.BlockSpec(memory_space=pl.ANY)
-    pairs, grads = pl.pallas_call(
-        functools.partial(exchange, n),
-        out_shape=[jax.ShapeDtypeStruct((n, chunk, width), BF16)] * 2,
-        in_specs=[hbm] * 2,
-        out_specs=[vmem] * 2,
+    hbm = pl.BlockSpec(memory_space=pltpu.HBM)
+    anywhere = pl.BlockSpec(memory_space=pl.ANY)
+    shapes = [
+        jax.ShapeDtypeStruct(pair.shape, BF16),
+        jax.ShapeDtypeStruct(w_qkvg.shape, F32),
+        jax.ShapeDtypeStruct(w_out.shape, F32),
+        jax.ShapeDtypeStruct((heads, width), F32),
+        jax.ShapeDtypeStruct((1, width), F32),
+    ]
+    results = pl.pallas_call(
+        functools.partial(whole_crop, n, local),
+        out_shape=shapes,
+        in_specs=[hbm] * 6,
+        out_specs=[vmem] * 5,
         scratch_shapes=[
+            pltpu.VMEM((n, chunk, width), BF16),
+            pltpu.VMEM((n, chunk, width), BF16),
+            pltpu.VMEM(w_qkvg.shape, BF16),
+            pltpu.VMEM(w_out.shape, BF16),
+            pltpu.VMEM((heads, width), BF16),
+            pltpu.VMEM((1, width), F32),
+            pltpu.VMEM((cells, width), F32),
+            pltpu.VMEM((cells, width), F32),
+            pltpu.VMEM((cells, width), F32),
             pltpu.SemaphoreType.DMA((2, n)),
             pltpu.SemaphoreType.DMA((2, n)),
-            pltpu.SemaphoreType.DMA((2,)),
+            pltpu.SemaphoreType.DMA((6,)),
         ],
-        compiler_params=pltpu.CompilerParams(collective_id=0, has_side_effects=True),
-    )(pair.reshape(chunk, width), out_grad.reshape(chunk, width))
-    d_pair, d_qkvg, d_wout, d_wbias, d_gain = pl.pallas_call(
-        functools.partial(whole_crop, local),
-        out_shape=[
-            jax.ShapeDtypeStruct(pair.shape, BF16),
-            jax.ShapeDtypeStruct(w_qkvg.shape, F32),
-            jax.ShapeDtypeStruct(w_out.shape, F32),
-            jax.ShapeDtypeStruct((heads, width), F32),
-            jax.ShapeDtypeStruct((1, width), F32),
-        ],
-        in_specs=[vmem] * 6,
-        out_specs=[vmem] * 5,
-        scratch_shapes=[pltpu.VMEM((cells, width), F32)] * 3,
-        compiler_params=pltpu.CompilerParams(vmem_limit_bytes=32 * 1024 * 1024),
-    )(pairs, grads, w_qkvg, w_out, w_bias.T, gain.reshape(1, width))
+        compiler_params=pltpu.CompilerParams(
+            collective_id=0, has_side_effects=True, vmem_limit_bytes=VMEM_LIMIT
+        ),
+    )(
+        pair.reshape(chunk, width),
+        out_grad.reshape(chunk, width),
+        w_qkvg,
+        w_out,
+        w_bias.T,
+        gain.reshape(1, width),
+    )
+    results = pl.pallas_call(
+        functools.partial(deliver, len(shapes)),
+        out_shape=shapes,
+        in_specs=[anywhere] * len(shapes),
+        out_specs=[hbm] * len(shapes),
+        scratch_shapes=[pltpu.SemaphoreType.DMA((len(shapes),))],
+        compiler_params=pltpu.CompilerParams(vmem_limit_bytes=VMEM_LIMIT),
+    )(*results)
+    d_pair, d_qkvg, d_wout, d_wbias, d_gain = results
     return (d_pair, d_qkvg, d_wout, d_wbias.T, d_gain.reshape(width))
 
 

time: 19.3 us -> 25.5 us (1.32)
  Pallas kernels: 14.4 us -> 24.7 us
  local copies, waits for them, and re-layouts: 4.01 us -> 0 us
    pallas_call x2, Pallas kernels: 14.4 us -> 24.7 us  [the longest x1 13.3 us: gathered_plan(): pl.pallas_call(functools.partial(whole_crop, n, local), out_shape=shapes,...]
    unnamed x12 -> x0, local copies, waits for them, and re-layouts: 4.01 us -> none
where the time goes in v2:
time: 25.5 us; the launch traced here: 25.4 us
  Pallas kernels  24.7 us (97%)
  between operations  0.64 us (3%)
    pallas_call x1, Pallas kernels, gathered_plan(): pl.pallas_call(functools.partial(whole_crop, n, local), out_shape=shapes,...  13.3 us
    pallas_call x1, Pallas kernels, gathered_plan(): pl.pallas_call(functools.partial(deliver, len(shapes)), out_shape=shapes,...  11.4 us

profile of v2, /device:TPU:0, one launch (start us, length us, event | category | flops | bytes accessed | tf_op | source)
XLA Modules:
  0.0 25.4 jit_solution(2501548110812142572)
XLA Ops:
  0.6 13.3 %shard_map.101 = (bf16[2,16,128]{2,1,0:T(8,128)(2,1)}, f32[128,512]{1,0:T(8,128)}, f32[128,128]{1,0:T(8,128)}, f32[4,128]{1,0:T(4,128)}, f32[1,128]{1,0:T(1,128)}) custom-call(bf16[32,128]{1,0:T(8,128)(2,1)} %bitcast.6, bf16[32,128]{1,0:T(8,128)(2,1)} %bitcast.7, bf16[128,512]{1,0:T(8,128)(2,1)} %w_qkvg_hbm.1, bf16[128,128]{1,0:T(8,128)(2,1)} %w_out_hbm.1, ...), custom_call_target="tpu_custom_call" | custom-call | tf_op jit(solution)/shard_map/pallas_call | solution.py:402
  14.0 11.4 %shard_map.102 = (bf16[2,16,128]{2,1,0:T(8,128)(2,1)}, f32[128,512]{1,0:T(8,128)}, f32[128,128]{1,0:T(8,128)}, f32[4,128]{1,0:T(4,128)}, f32[1,128]{1,0:T(1,128)}) custom-call(bf16[2,16,128]{2,1,0:T(8,128)(2,1)} %get-tuple-element.15.refs_0_, f32[128,512]{1,0:T(8,128)} %get-tuple-element.16.refs_1_, f32[128,128]{1,0:T(8,128)} %get-tuple-element.17.refs_2_, ...), custom_call_target="tpu_custom_call" | custom-call | tf_op jit(solution)/shard_map/pallas_call | solution.py:432

commit v3 on v2

--- a/solution.py
+++ b/solution.py
@@ -133,6 +133,7 @@
 
 
 BLOCK = 128
+PIECE = 32
 VMEM_LIMIT = 60 * 1024 * 1024
 MASKED = -1e30
 BF16 = jnp.bfloat16
@@ -190,22 +191,24 @@
         for index, (src, dst) in enumerate(
             (
                 (pair_hbm, pairs_ref.at[me]),
+                (grad_hbm, grads_ref.at[me]),
                 (gain_hbm, gain_ref),
                 (w_qkvg_hbm, w_qkvg_ref),
                 (w_bias_hbm, w_bias_ref),
-                (grad_hbm, grads_ref.at[me]),
                 (w_out_hbm, w_out_ref),
             )
         )
     ]
     for copy in staged:
         copy.start()
+    staged[0].wait()
+    staged[1].wait()
     pl.semaphore_wait(barrier, n - 1)
     sent = []
-    for kind, (src, dst) in enumerate(((pair_hbm, pairs_ref), (grad_hbm, grads_ref))):
+    for kind, dst in enumerate((pairs_ref, grads_ref)):
         for offset in range(1, n):
             copy = pltpu.make_async_remote_copy(
-                src_ref=src,
+                src_ref=dst.at[me],
                 dst_ref=dst.at[me],
                 send_sem=send_sems.at[kind, offset],
                 recv_sem=recv_sems.at[kind, offset],
@@ -253,7 +256,7 @@
             out = jnp.where(lane_head == h, stacked[h * BLOCK : (h + 1) * BLOCK], out)
         return out
 
-    for copy in staged[:4]:
+    for copy in staged[2:5]:
         copy.wait()
     for copy in sent[: n - 1]:
         copy.wait_recv()
@@ -311,7 +314,7 @@
         attended = mm(flat_b, vals, (0, 0))
         forward.append((queries, keys, vals, gate, probs, probs_b, attended))
 
-    for copy in staged[4:]:
+    for copy in staged[5:]:
         copy.wait()
     for copy in sent[n - 1 :]:
         copy.wait_recv()
@@ -374,14 +377,28 @@
 
 
 def deliver(count, *refs):
-    copies = [
-        pltpu.make_async_copy(refs[index], refs[count + index], refs[-1].at[index])
-        for index in range(count)
+    ins, outs, held = refs[:count], refs[count : 2 * count], refs[2 * count : 3 * count]
+    in_sems, out_sems = refs[3 * count :]
+    pieces = []
+    for index in range(count):
+        rows = ins[index].shape[0]
+        step = min(rows, PIECE)
+        pieces += [(index, pl.ds(start, step)) for start in range(0, rows, step)]
+    loads = [
+        pltpu.make_async_copy(ins[index].at[rows], held[index].at[rows], in_sems.at[piece])
+        for piece, (index, rows) in enumerate(pieces)
     ]
-    for copy in copies:
-        copy.start()
-    for copy in copies:
-        copy.wait()
+    stores = [
+        pltpu.make_async_copy(held[index].at[rows], outs[index].at[rows], out_sems.at[piece])
+        for piece, (index, rows) in enumerate(pieces)
+    ]
+    for load in loads:
+        load.start()
+    for load, store in zip(loads, stores):
+        load.wait()
+        store.start()
+    for store in stores:
+        store.wait()
 
 
 def gathered_plan(n, pair, out_grad, w_qkvg, w_out, w_bias, gain):
@@ -429,12 +446,14 @@
         w_bias.T,
         gain.reshape(1, width),
     )
+    pieces = sum(-(-shape.shape[0] // PIECE) for shape in shapes)
     results = pl.pallas_call(
         functools.partial(deliver, len(shapes)),
         out_shape=shapes,
         in_specs=[anywhere] * len(shapes),
         out_specs=[hbm] * len(shapes),
-        scratch_shapes=[pltpu.SemaphoreType.DMA((len(shapes),))],
+        scratch_shapes=[pltpu.VMEM(shape.shape, shape.dtype) for shape in shapes]
+        + [pltpu.SemaphoreType.DMA((pieces,))] * 2,
         compiler_params=pltpu.CompilerParams(vmem_limit_bytes=VMEM_LIMIT),
     )(*results)
     d_pair, d_qkvg, d_wout, d_wbias, d_gain = results

time: 25.5 us -> 15.6 us (0.61)
  Pallas kernels: 24.7 us -> 14.7 us
    pallas_call x1, Pallas kernels: 11.4 us -> 1.79 us  [gathered_plan(): pl.pallas_call(functools.partial(deliver, len(shapes)), out_shape=shapes,...]
    pallas_call x1, Pallas kernels: 13.3 us -> 12.9 us  [gathered_plan(): pl.pallas_call(functools.partial(whole_crop, n, local), out_shape=shapes,...]
where the time goes in v3:
time: 15.6 us; the launch traced here: 15.3 us
  Pallas kernels  14.7 us (94%)
  between operations  0.64 us (4%)
    pallas_call x1, Pallas kernels, gathered_plan(): pl.pallas_call(functools.partial(whole_crop, n, local), out_shape=shapes,...  12.9 us
    pallas_call x1, Pallas kernels, gathered_plan(): pl.pallas_call(functools.partial(deliver, len(shapes)), out_shape=shapes,...  1.79 us

profile of v3, /device:TPU:0, one launch (start us, length us, event | category | flops | bytes accessed | tf_op | source)
XLA Modules:
  0.0 15.3 jit_solution(17896831869844837586)
XLA Ops:
  0.6 12.9 %shard_map.101 = (bf16[2,16,128]{2,1,0:T(8,128)(2,1)}, f32[128,512]{1,0:T(8,128)}, f32[128,128]{1,0:T(8,128)}, f32[4,128]{1,0:T(4,128)}, f32[1,128]{1,0:T(1,128)}) custom-call(bf16[32,128]{1,0:T(8,128)(2,1)} %bitcast.6, bf16[32,128]{1,0:T(8,128)(2,1)} %bitcast.7, bf16[128,512]{1,0:T(8,128)(2,1)} %w_qkvg_hbm.1, bf16[128,128]{1,0:T(8,128)(2,1)} %w_out_hbm.1, ...), custom_call_target="tpu_custom_call" | custom-call | tf_op jit(solution)/shard_map/pallas_call | solution.py:419
  13.6 1.8 %shard_map.102 = (bf16[2,16,128]{2,1,0:T(8,128)(2,1)}, f32[128,512]{1,0:T(8,128)}, f32[128,128]{1,0:T(8,128)}, f32[4,128]{1,0:T(4,128)}, f32[1,128]{1,0:T(1,128)}) custom-call(bf16[2,16,128]{2,1,0:T(8,128)(2,1)} %get-tuple-element.15.refs_0_, f32[128,512]{1,0:T(8,128)} %get-tuple-element.16.refs_1_, f32[128,128]{1,0:T(8,128)} %get-tuple-element.17.refs_2_, ...), custom_call_target="tpu_custom_call" | custom-call | tf_op jit(solution)/shard_map/pallas_call | solution.py:450

commit v4 on v2

--- a/solution.py
+++ b/solution.py
@@ -133,7 +133,7 @@
 
 
 BLOCK = 128
-VMEM_LIMIT = 60 * 1024 * 1024
+VMEM_LIMIT = 16 * 1024 * 1024
 MASKED = -1e30
 BF16 = jnp.bfloat16
 F32 = jnp.float32
@@ -190,22 +190,24 @@
         for index, (src, dst) in enumerate(
             (
                 (pair_hbm, pairs_ref.at[me]),
+                (grad_hbm, grads_ref.at[me]),
                 (gain_hbm, gain_ref),
                 (w_qkvg_hbm, w_qkvg_ref),
                 (w_bias_hbm, w_bias_ref),
-                (grad_hbm, grads_ref.at[me]),
                 (w_out_hbm, w_out_ref),
             )
         )
     ]
     for copy in staged:
         copy.start()
+    staged[0].wait()
+    staged[1].wait()
     pl.semaphore_wait(barrier, n - 1)
     sent = []
-    for kind, (src, dst) in enumerate(((pair_hbm, pairs_ref), (grad_hbm, grads_ref))):
+    for kind, dst in enumerate((pairs_ref, grads_ref)):
         for offset in range(1, n):
             copy = pltpu.make_async_remote_copy(
-                src_ref=src,
+                src_ref=dst.at[me],
                 dst_ref=dst.at[me],
                 send_sem=send_sems.at[kind, offset],
                 recv_sem=recv_sems.at[kind, offset],
@@ -253,7 +255,7 @@
             out = jnp.where(lane_head == h, stacked[h * BLOCK : (h + 1) * BLOCK], out)
         return out
 
-    for copy in staged[:4]:
+    for copy in staged[2:5]:
         copy.wait()
     for copy in sent[: n - 1]:
         copy.wait_recv()
@@ -311,7 +313,7 @@
         attended = mm(flat_b, vals, (0, 0))
         forward.append((queries, keys, vals, gate, probs, probs_b, attended))
 
-    for copy in staged[4:]:
+    for copy in staged[5:]:
         copy.wait()
     for copy in sent[n - 1 :]:
         copy.wait_recv()
@@ -391,7 +393,6 @@
     chunk = local * length
     vmem = pl.BlockSpec(memory_space=pltpu.VMEM)
     hbm = pl.BlockSpec(memory_space=pltpu.HBM)
-    anywhere = pl.BlockSpec(memory_space=pl.ANY)
     shapes = [
         jax.ShapeDtypeStruct(pair.shape, BF16),
         jax.ShapeDtypeStruct(w_qkvg.shape, F32),
@@ -399,9 +400,17 @@
         jax.ShapeDtypeStruct((heads, width), F32),
         jax.ShapeDtypeStruct((1, width), F32),
     ]
+    operands = (
+        pair.reshape(chunk, width),
+        out_grad.reshape(chunk, width),
+        w_qkvg,
+        w_out,
+        w_bias.T,
+        gain.reshape(1, width),
+    )
     results = pl.pallas_call(
         functools.partial(whole_crop, n, local),
-        out_shape=shapes,
+        out_shape=[pltpu.VMEM(shape.shape, shape.dtype) for shape in shapes],
         in_specs=[hbm] * 6,
         out_specs=[vmem] * 5,
         scratch_shapes=[
@@ -421,18 +430,11 @@
         compiler_params=pltpu.CompilerParams(
             collective_id=0, has_side_effects=True, vmem_limit_bytes=VMEM_LIMIT
         ),
-    )(
-        pair.reshape(chunk, width),
-        out_grad.reshape(chunk, width),
-        w_qkvg,
-        w_out,
-        w_bias.T,
-        gain.reshape(1, width),
-    )
+    )(*[pltpu.with_memory_space_constraint(value, pltpu.HBM) for value in operands])
     results = pl.pallas_call(
         functools.partial(deliver, len(shapes)),
         out_shape=shapes,
-        in_specs=[anywhere] * len(shapes),
+        in_specs=[vmem] * len(shapes),
         out_specs=[hbm] * len(shapes),
         scratch_shapes=[pltpu.SemaphoreType.DMA((len(shapes),))],
         compiler_params=pltpu.CompilerParams(vmem_limit_bytes=VMEM_LIMIT),

time: 25.5 us -> 13.8 us (0.54)
  Pallas kernels: 24.7 us -> 13 us
    pallas_call x1, Pallas kernels: 11.4 us -> 0.77 us  [gathered_plan(): pl.pallas_call(functools.partial(deliver, len(shapes)), out_shape=shapes,...]
    pallas_call x1, Pallas kernels: 13.3 us -> 12.2 us  [gathered_plan(): pl.pallas_call(functools.partial(whole_crop, n, local), out_shape=[pltpu....]
where the time goes in v4:
time: 13.8 us; the launch traced here: 13.6 us
  Pallas kernels  13 us (94%)
  between operations  0.64 us (5%)
    pallas_call x1, Pallas kernels, gathered_plan(): pl.pallas_call(functools.partial(whole_crop, n, local), out_shape=[pltpu....  12.2 us
    pallas_call x1, Pallas kernels, gathered_plan(): pl.pallas_call(functools.partial(deliver, len(shapes)), out_shape=shapes,...  0.77 us

profile of v4, /device:TPU:0, one launch (start us, length us, event | category | flops | bytes accessed | tf_op | source)
XLA Modules:
  0.0 13.6 jit_solution(10463691368197071790)
XLA Ops:
  0.6 12.2 %shard_map.101 = (bf16[2,16,128]{2,1,0:T(8,128)(2,1)S(1)}, f32[128,512]{1,0:T(8,128)S(1)}, f32[128,128]{1,0:T(8,128)S(1)}, f32[4,128]{1,0:T(4,128)S(1)}, f32[1,128]{1,0:T(1,128)S(1)}) custom-call(bf16[32,128]{1,0:T(8,128)(2,1)} %bitcast.6, bf16[32,128]{1,0:T(8,128)(2,1)} %bitcast.7, bf16[128,512]{1,0:T(8,128)(2,1)} %w_qkvg_hbm.1, ...), custom_call_target="tpu_custom_call" | custom-call | tf_op jit(solution)/shard_map/pallas_call | solution.py:411
  12.8 0.8 %shard_map.102 = (bf16[2,16,128]{2,1,0:T(8,128)(2,1)}, f32[128,512]{1,0:T(8,128)}, f32[128,128]{1,0:T(8,128)}, f32[4,128]{1,0:T(4,128)}, f32[1,128]{1,0:T(1,128)}) custom-call(bf16[2,16,128]{2,1,0:T(8,128)(2,1)S(1)} %get-tuple-element.15.refs_0_, f32[128,512]{1,0:T(8,128)S(1)} %get-tuple-element.16.refs_1_, f32[128,128]{1,0:T(8,128)S(1)} %get-tuple-element.17.refs_2_, ...), custom_call_target="tpu_custom_call" | custom-call | tf_op jit(solution)/shard_map/pallas_call | solution.py:434

commit v5 on v4

--- a/solution.py
+++ b/solution.py
@@ -149,6 +149,15 @@
     return value.bit_length() - 1
 
 
+def partner(me, step):
+    other = me
+    for bit in range(log2(step) + 1):
+        weight = 1 << bit
+        if step & weight:
+            other = other + weight * (1 - 2 * lax.rem(me // weight, 2))
+    return other
+
+
 def whole_crop(
     n,
     local,
@@ -158,31 +167,32 @@
     w_out_hbm,
     w_bias_hbm,
     gain_hbm,
-    d_pair_ref,
-    d_qkvg_ref,
-    d_wout_ref,
+    tokens_ref,
+    d_proj_ref,
+    mixed_ref,
+    grads_ref,
+    d_bias_x_ref,
+    normed_ref,
+    inv_ref,
+    w_qkvg_ref,
+    gain_ref,
+    restore_ref,
     d_wbias_ref,
-    d_gain_ref,
     pairs_ref,
-    grads_ref,
-    w_qkvg_ref,
     w_out_ref,
     w_bias_ref,
-    gain_ref,
-    d_xn_ref,
-    normed_ref,
-    inv_ref,
     send_sems,
     recv_sems,
     local_sems,
 ):
     me = lax.axis_index("row")
+    partners = {step: partner(me, step) for step in range(1, n)}
     barrier = pltpu.get_barrier_semaphore()
-    for offset in range(1, n):
+    for step in partners:
         pl.semaphore_signal(
             barrier,
             inc=1,
-            device_id={"row": lax.rem(me + offset, n)},
+            device_id={"row": partners[step]},
             device_id_type=pl.DeviceIdType.MESH,
         )
     staged = [
@@ -205,13 +215,13 @@
     pl.semaphore_wait(barrier, n - 1)
     sent = []
     for kind, dst in enumerate((pairs_ref, grads_ref)):
-        for offset in range(1, n):
+        for step in reversed(range(1, n)):
             copy = pltpu.make_async_remote_copy(
                 src_ref=dst.at[me],
                 dst_ref=dst.at[me],
-                send_sem=send_sems.at[kind, offset],
-                recv_sem=recv_sems.at[kind, offset],
-                device_id={"row": lax.rem(me + offset, n)},
+                send_sem=send_sems.at[kind, step],
+                recv_sem=recv_sems.at[kind, step],
+                device_id={"row": partners[step]},
                 device_id_type=pl.DeviceIdType.MESH,
             )
             copy.start()
@@ -236,6 +246,9 @@
     g, r = iota((cells, cells), 0), iota((cells, cells), 1)
     cell = (row_of(g) << s_length) + ((g >> s_chunk) << s_local) + (g & (local - 1))
     permute = (cell == r).astype(F32).astype(BF16)
+    r, g = iota((cells, cells), 0), iota((cells, cells), 1)
+    cell = (row_of(g) << s_length) + ((g >> s_chunk) << s_local) + (g & (local - 1))
+    restore_ref[...] = (cell == r).astype(F32).astype(BF16)
     p, q = iota((BLOCK, BLOCK), 0), iota((BLOCK, BLOCK), 1)
     same_column = ((p >> s_chunk) == (q >> s_chunk)) & (((p ^ q) & (local - 1)) == 0)
     p, r = iota((BLOCK, cells), 0), iota((BLOCK, cells), 1)
@@ -277,6 +290,7 @@
     inv_ref[...] = jnp.broadcast_to(inv_std, (cells, width))
 
     tokens = mm(permute, xn).astype(BF16)
+    tokens_ref[...] = tokens
     proj = mm(tokens, w_qkvg)
     bias_cells = mm(xn, w_bias_rows, (1, 1))
     bias = mm(
@@ -307,7 +321,7 @@
         scores = scores.reshape(heads, BLOCK, BLOCK)
         top = jnp.max(scores, axis=1, keepdims=True)
         weights = jnp.exp(scores - top)
-        probs = weights / jnp.sum(weights, axis=1, keepdims=True)
+        probs = weights * (1.0 / jnp.sum(weights, axis=1, keepdims=True))
         probs_b = probs.astype(BF16)
         flat_b = probs_b.reshape(heads * BLOCK, BLOCK)
         attended = mm(flat_b, vals, (0, 0))
@@ -320,7 +334,6 @@
     grads = grads_ref[...].reshape(cells, width)
     d_mixed_all = mm(grads, w_out_ref[...], (1, 1))
 
-    mixed_parts, d_proj_parts = [], []
     d_bias_x = jnp.zeros((cells, width), F32)
     d_wbias = jnp.zeros((heads * BLOCK, width), F32)
     for start in range(0, cells, BLOCK):
@@ -328,7 +341,7 @@
         rows = slice(start, start + BLOCK)
         flat_b = probs_b.reshape(heads * BLOCK, BLOCK)
         d_mixed = d_mixed_all[rows]
-        mixed_parts.append((gate * attended).astype(BF16))
+        mixed_ref[rows, :] = (gate * attended).astype(BF16)
         d_gate = d_mixed * attended * gate * (1.0 - gate)
         d_att = (d_mixed * gate).astype(BF16)
         d_values = own_head(mm(flat_b, d_att))
@@ -338,9 +351,8 @@
         flat_d = d_scores.reshape(heads * BLOCK, BLOCK)
         d_queries = mm(flat_d, keys, (0, 0)) * scale
         d_keys = own_head(mm(flat_d, queries)) * scale
-        d_proj_parts.append(
-            jnp.concatenate([d_queries, d_keys, d_values, d_gate], 1).astype(BF16)
-        )
+        for index, part in enumerate((d_queries, d_keys, d_values, d_gate)):
+            d_proj_ref[rows, index * width : (index + 1) * width] = part.astype(BF16)
         terms = mm(pick_key, jnp.concatenate([d_scores[h] for h in range(heads)], 1))
         terms = jnp.concatenate(
             [
@@ -352,16 +364,64 @@
         d_bias_x = d_bias_x + mm(terms, w_bias_rows)
         d_wbias = d_wbias + mm(terms, xn, (0, 0))
 
-    d_proj = jnp.concatenate(d_proj_parts, 0)
-    mixed = jnp.concatenate(mixed_parts, 0)
-    d_qkvg_ref[...] = mm(tokens, d_proj, (0, 0)) * inv_count
-    d_wout_ref[...] = mm(mixed, grads, (0, 0)) * inv_count
+    d_bias_x_ref[...] = d_bias_x.astype(BF16)
     d_wbias_ref[...] = jnp.sum(d_wbias.reshape(heads, BLOCK, width), axis=1) * inv_count
-    d_tokens = mm(d_proj, w_qkvg, (1, 1)).astype(BF16)
-    d_xn = mm(permute, d_tokens, (0, 0)) + d_bias_x.astype(BF16).astype(F32)
-    d_gain_ref[...] = jnp.sum(d_xn * normed, axis=0, keepdims=True) * inv_count
+    for copy in sent:
+        copy.wait_send()
+
+
+def finish(
+    inv_count,
+    tokens_ref,
+    d_proj_ref,
+    mixed_ref,
+    grads_ref,
+    d_bias_x_ref,
+    normed_ref,
+    inv_ref,
+    w_qkvg_ref,
+    gain_ref,
+    restore_ref,
+    d_wbias_ref,
+    d_pair_hbm,
+    d_qkvg_hbm,
+    d_wout_hbm,
+    d_wbias_hbm,
+    d_gain_hbm,
+    d_pair_ref,
+    d_qkvg_ref,
+    d_wout_ref,
+    d_gain_ref,
+    d_xn_ref,
+    sems,
+):
+    me = lax.axis_index("row")
+    chunk = grads_ref.shape[1]
+    copies = [
+        pltpu.make_async_copy(src, dst, sems.at[index])
+        for index, (src, dst) in enumerate(
+            (
+                (d_wbias_ref, d_wbias_hbm),
+                (d_qkvg_ref, d_qkvg_hbm),
+                (d_wout_ref, d_wout_hbm),
+                (d_gain_ref, d_gain_hbm),
+                (d_pair_ref, d_pair_hbm),
+            )
+        )
+    ]
+    copies[0].start()
+    d_proj = d_proj_ref[...]
+    gain = gain_ref[...]
+    d_qkvg_ref[...] = mm(tokens_ref[...], d_proj, (0, 0)) * inv_count
+    copies[1].start()
+    grads = grads_ref[...].reshape(mixed_ref.shape)
+    d_wout_ref[...] = mm(mixed_ref[...], grads, (0, 0)) * inv_count
+    copies[2].start()
+    d_tokens = mm(d_proj, w_qkvg_ref[...], (1, 1)).astype(BF16)
+    d_xn = mm(restore_ref[...], d_tokens) + d_bias_x_ref[...].astype(F32)
     d_xn_ref[...] = d_xn
-
+    d_gain_ref[...] = jnp.sum(d_xn * normed_ref[...], axis=0, keepdims=True) * inv_count
+    copies[3].start()
     own = pl.ds(pl.multiple_of(me * chunk, chunk), chunk)
     normed = normed_ref[own, :]
     scaled = d_xn_ref[own, :] * gain
@@ -371,17 +431,7 @@
         - normed * jnp.mean(scaled * normed, axis=-1, keepdims=True)
     )
     d_pair_ref[...] = d_pair.astype(BF16).reshape(d_pair_ref.shape)
-    for copy in sent:
-        copy.wait_send()
-
-
-def deliver(count, *refs):
-    copies = [
-        pltpu.make_async_copy(refs[index], refs[count + index], refs[-1].at[index])
-        for index in range(count)
-    ]
-    for copy in copies:
-        copy.start()
+    copies[4].start()
     for copy in copies:
         copy.wait()
 
@@ -408,37 +458,51 @@
         w_bias.T,
         gain.reshape(1, width),
     )
-    results = pl.pallas_call(
+    passed = [
+        pltpu.VMEM((cells, width), BF16),
+        pltpu.VMEM((cells, w_qkvg.shape[1]), BF16),
+        pltpu.VMEM((cells, width), BF16),
+        pltpu.VMEM((n, chunk, width), BF16),
+        pltpu.VMEM((cells, width), BF16),
+        pltpu.VMEM((cells, width), F32),
+        pltpu.VMEM((cells, width), F32),
+        pltpu.VMEM(w_qkvg.shape, BF16),
+        pltpu.VMEM((1, width), F32),
+        pltpu.VMEM((cells, cells), BF16),
+        pltpu.VMEM((heads, width), F32),
+    ]
+    halfway = pl.pallas_call(
         functools.partial(whole_crop, n, local),
-        out_shape=[pltpu.VMEM(shape.shape, shape.dtype) for shape in shapes],
-        in_specs=[hbm] * 6,
-        out_specs=[vmem] * 5,
+        out_shape=passed,
+        in_specs=[hbm] * len(operands),
+        out_specs=[vmem] * len(passed),
         scratch_shapes=[
             pltpu.VMEM((n, chunk, width), BF16),
-            pltpu.VMEM((n, chunk, width), BF16),
-            pltpu.VMEM(w_qkvg.shape, BF16),
             pltpu.VMEM(w_out.shape, BF16),
             pltpu.VMEM((heads, width), BF16),
-            pltpu.VMEM((1, width), F32),
-            pltpu.VMEM((cells, width), F32),
-            pltpu.VMEM((cells, width), F32),
-            pltpu.VMEM((cells, width), F32),
             pltpu.SemaphoreType.DMA((2, n)),
             pltpu.SemaphoreType.DMA((2, n)),
-            pltpu.SemaphoreType.DMA((6,)),
+            pltpu.SemaphoreType.DMA((len(operands),)),
         ],
         compiler_params=pltpu.CompilerParams(
             collective_id=0, has_side_effects=True, vmem_limit_bytes=VMEM_LIMIT
         ),
     )(*[pltpu.with_memory_space_constraint(value, pltpu.HBM) for value in operands])
     results = pl.pallas_call(
-        functools.partial(deliver, len(shapes)),
+        functools.partial(finish, 1.0 / length),
         out_shape=shapes,
-        in_specs=[vmem] * len(shapes),
+        in_specs=[vmem] * len(passed),
         out_specs=[hbm] * len(shapes),
-        scratch_shapes=[pltpu.SemaphoreType.DMA((len(shapes),))],
+        scratch_shapes=[
+            pltpu.VMEM(pair.shape, BF16),
+            pltpu.VMEM(w_qkvg.shape, F32),
+            pltpu.VMEM(w_out.shape, F32),
+            pltpu.VMEM((1, width), F32),
+            pltpu.VMEM((cells, width), F32),
+            pltpu.SemaphoreType.DMA((len(shapes),)),
+        ],
         compiler_params=pltpu.CompilerParams(vmem_limit_bytes=VMEM_LIMIT),
-    )(*results)
+    )(*halfway)
     d_pair, d_qkvg, d_wout, d_wbias, d_gain = results
     return (d_pair, d_qkvg, d_wout, d_wbias.T, d_gain.reshape(width))
 
@@ -446,7 +510,7 @@
 def per_device(n, pair, out_grad, w_qkvg, w_out, w_bias, gain):
     local, length, width = pair.shape
     chunk = local * length
-    powers = all(size & (size - 1) == 0 for size in (local, length, width, w_bias.shape[1]))
+    powers = all(size & (size - 1) == 0 for size in (n, local, length, width, w_bias.shape[1]))
     fits = n > 1 and width == BLOCK and chunk % 16 == 0 and BLOCK % chunk == 0
     if powers and fits and length * length % BLOCK == 0 and length <= 32:
         return gathered_plan(n, pair, out_grad, w_qkvg, w_out, w_bias, gain)

time: 13.8 us -> 14.6 us (1.058)
  Pallas kernels: 13 us -> 13.7 us
    pallas_call x2, Pallas kernels: 13 us -> 13.7 us  [the longest x1 12.5 us: gathered_plan(): pl.pallas_call(functools.partial(whole_crop, n, local), out_shape=passed,...]
where the time goes in v5:
time: 14.6 us; the launch traced here: 14.4 us
  Pallas kernels  13.7 us (94%)
  between operations  0.64 us (4%)
    pallas_call x1, Pallas kernels, gathered_plan(): pl.pallas_call(functools.partial(whole_crop, n, local), out_shape=passed,...  12.5 us
    pallas_call x1, Pallas kernels, gathered_plan(): pl.pallas_call(functools.partial(finish, 1.0 / length), out_shape=shapes,...  1.26 us

profile of v5, /device:TPU:0, one launch (start us, length us, event | category | flops | bytes accessed | tf_op | source)
XLA Modules:
  0.0 14.4 jit_solution(9083855473714348621)
XLA Ops:
  0.6 12.5 %shard_map.101 = (bf16[256,128]{1,0:T(8,128)(2,1)S(1)}, bf16[256,512]{1,0:T(8,128)(2,1)S(1)}, bf16[256,128]{1,0:T(8,128)(2,1)S(1)}, bf16[8,32,128]{2,1,0:T(8,128...) custom-call(bf16[32,128]{1,0:T(8,128)(2,1)} %bitcast.6, ...), custom_call_target="tpu_custom_call" | custom-call | tf_op jit(solution)/shard_map/pallas_call | solution.py:474
  13.1 1.3 %shard_map.102 = (bf16[2,16,128]{2,1,0:T(8,128)(2,1)}, f32[128,512]{1,0:T(8,128)}, f32[128,128]{1,0:T(8,128)}, f32[4,128]{1,0:T(4,128)}, f32[1,128]{1,0:T(1,128)}) custom-call(bf16[256,128]{1,0:T(8,128)(2,1)S(1)} %get-tuple-element.21.tokens_ref, bf16[256,512]{1,0:T(8,128)(2,1)S(1)} %get-tuple-element.22.d_proj_ref, ...), custom_call_target="tpu_custom_call" | custom-call | tf_op jit(solution)/shard_map/pallas_call | solution.py:491

commit v6 on v4

--- a/solution.py
+++ b/solution.py
@@ -177,15 +177,7 @@
     local_sems,
 ):
     me = lax.axis_index("row")
-    barrier = pltpu.get_barrier_semaphore()
-    for offset in range(1, n):
-        pl.semaphore_signal(
-            barrier,
-            inc=1,
-            device_id={"row": lax.rem(me + offset, n)},
-            device_id_type=pl.DeviceIdType.MESH,
-        )
-    staged = [
+    loads = [
         pltpu.make_async_copy(src, dst, local_sems.at[index])
         for index, (src, dst) in enumerate(
             (
@@ -198,17 +190,24 @@
             )
         )
     ]
-    for copy in staged:
-        copy.start()
-    staged[0].wait()
-    staged[1].wait()
+    loads[0].start()
+    loads[1].start()
+    barrier = pltpu.get_barrier_semaphore()
+    for offset in range(1, n):
+        pl.semaphore_signal(
+            barrier,
+            inc=1,
+            device_id={"row": lax.rem(me + offset, n)},
+            device_id_type=pl.DeviceIdType.MESH,
+        )
     pl.semaphore_wait(barrier, n - 1)
     sent = []
-    for kind, dst in enumerate((pairs_ref, grads_ref)):
+    for kind, blocks in enumerate((pairs_ref, grads_ref)):
+        loads[kind].wait()
         for offset in range(1, n):
             copy = pltpu.make_async_remote_copy(
-                src_ref=dst.at[me],
-                dst_ref=dst.at[me],
+                src_ref=blocks.at[me],
+                dst_ref=blocks.at[me],
                 send_sem=send_sems.at[kind, offset],
                 recv_sem=recv_sems.at[kind, offset],
                 device_id={"row": lax.rem(me + offset, n)},
@@ -216,6 +215,9 @@
             )
             copy.start()
             sent.append(copy)
+        if kind == 0:
+            for copy in loads[2:]:
+                copy.start()
 
     chunk = pairs_ref.shape[1]
     width = pairs_ref.shape[2]
@@ -236,6 +238,9 @@
     g, r = iota((cells, cells), 0), iota((cells, cells), 1)
     cell = (row_of(g) << s_length) + ((g >> s_chunk) << s_local) + (g & (local - 1))
     permute = (cell == r).astype(F32).astype(BF16)
+    r, g = iota((cells, cells), 0), iota((cells, cells), 1)
+    cell = (row_of(g) << s_length) + ((g >> s_chunk) << s_local) + (g & (local - 1))
+    restore = (cell == r).astype(F32).astype(BF16)
     p, q = iota((BLOCK, BLOCK), 0), iota((BLOCK, BLOCK), 1)
     same_column = ((p >> s_chunk) == (q >> s_chunk)) & (((p ^ q) & (local - 1)) == 0)
     p, r = iota((BLOCK, cells), 0), iota((BLOCK, cells), 1)
@@ -255,7 +260,7 @@
             out = jnp.where(lane_head == h, stacked[h * BLOCK : (h + 1) * BLOCK], out)
         return out
 
-    for copy in staged[2:5]:
+    for copy in loads[2:5]:
         copy.wait()
     for copy in sent[: n - 1]:
         copy.wait_recv()
@@ -307,13 +312,13 @@
         scores = scores.reshape(heads, BLOCK, BLOCK)
         top = jnp.max(scores, axis=1, keepdims=True)
         weights = jnp.exp(scores - top)
-        probs = weights / jnp.sum(weights, axis=1, keepdims=True)
+        probs = weights * (1.0 / jnp.sum(weights, axis=1, keepdims=True))
         probs_b = probs.astype(BF16)
         flat_b = probs_b.reshape(heads * BLOCK, BLOCK)
         attended = mm(flat_b, vals, (0, 0))
         forward.append((queries, keys, vals, gate, probs, probs_b, attended))
 
-    for copy in staged[5:]:
+    for copy in loads[5:]:
         copy.wait()
     for copy in sent[n - 1 :]:
         copy.wait_recv()
@@ -358,7 +363,7 @@
     d_wout_ref[...] = mm(mixed, grads, (0, 0)) * inv_count
     d_wbias_ref[...] = jnp.sum(d_wbias.reshape(heads, BLOCK, width), axis=1) * inv_count
     d_tokens = mm(d_proj, w_qkvg, (1, 1)).astype(BF16)
-    d_xn = mm(permute, d_tokens, (0, 0)) + d_bias_x.astype(BF16).astype(F32)
+    d_xn = mm(restore, d_tokens) + d_bias_x.astype(BF16).astype(F32)
     d_gain_ref[...] = jnp.sum(d_xn * normed, axis=0, keepdims=True) * inv_count
     d_xn_ref[...] = d_xn
 

time: 13.8 us -> 13.7 us (level)
  no operation moved by 1% of the time
where the time goes in v6:
time: 13.7 us; the launch traced here: 13.5 us
  Pallas kernels  12.9 us (94%)
  between operations  0.64 us (5%)
    pallas_call x1, Pallas kernels, gathered_plan(): pl.pallas_call(functools.partial(whole_crop, n, local), out_shape=[pltpu....  12.1 us
    pallas_call x1, Pallas kernels, gathered_plan(): pl.pallas_call(functools.partial(deliver, len(shapes)), out_shape=shapes,...  0.77 us

profile of v6, /device:TPU:0, one launch (start us, length us, event | category | flops | bytes accessed | tf_op | source)
XLA Modules:
  0.0 13.5 jit_solution(14617437874726899283)
XLA Ops:
  0.6 12.1 %shard_map.101 = (bf16[2,16,128]{2,1,0:T(8,128)(2,1)S(1)}, f32[128,512]{1,0:T(8,128)S(1)}, f32[128,128]{1,0:T(8,128)S(1)}, f32[4,128]{1,0:T(4,128)S(1)}, f32[1,128]{1,0:T(1,128)S(1)}) custom-call(bf16[32,128]{1,0:T(8,128)(2,1)} %bitcast.6, bf16[32,128]{1,0:T(8,128)(2,1)} %bitcast.7, bf16[128,512]{1,0:T(8,128)(2,1)} %w_qkvg_hbm.1, ...), custom_call_target="tpu_custom_call" | custom-call | tf_op jit(solution)/shard_map/pallas_call | solution.py:416
  12.7 0.8 %shard_map.102 = (bf16[2,16,128]{2,1,0:T(8,128)(2,1)}, f32[128,512]{1,0:T(8,128)}, f32[128,128]{1,0:T(8,128)}, f32[4,128]{1,0:T(4,128)}, f32[1,128]{1,0:T(1,128)}) custom-call(bf16[2,16,128]{2,1,0:T(8,128)(2,1)S(1)} %get-tuple-element.15.refs_0_, f32[128,512]{1,0:T(8,128)S(1)} %get-tuple-element.16.refs_1_, f32[128,128]{1,0:T(8,128)S(1)} %get-tuple-element.17.refs_2_, ...), custom_call_target="tpu_custom_call" | custom-call | tf_op jit(solution)/shard_map/pallas_call | solution.py:439

commit v7 on v6

--- a/solution.py
+++ b/solution.py
@@ -204,7 +204,7 @@
     sent = []
     for kind, blocks in enumerate((pairs_ref, grads_ref)):
         loads[kind].wait()
-        for offset in range(1, n):
+        for offset in sorted(range(1, n), key=lambda offset: min(offset, n - offset)):
             copy = pltpu.make_async_remote_copy(
                 src_ref=blocks.at[me],
                 dst_ref=blocks.at[me],

time: 13.7 us -> 14.3 us (1.044)
  Pallas kernels: 12.9 us -> 13.5 us
    pallas_call x1, Pallas kernels: 12.1 us -> 12.8 us  [gathered_plan(): pl.pallas_call(functools.partial(whole_crop, n, local), out_shape=[pltpu....]
where the time goes in v7:
time: 14.3 us; the launch traced here: 14.2 us
  Pallas kernels  13.5 us (94%)
  between operations  0.64 us (4%)
    pallas_call x1, Pallas kernels, gathered_plan(): pl.pallas_call(functools.partial(whole_crop, n, local), out_shape=[pltpu....  12.8 us
    pallas_call x1, Pallas kernels, gathered_plan(): pl.pallas_call(functools.partial(deliver, len(shapes)), out_shape=shapes,...  0.77 us

profile of v7, /device:TPU:0, one launch (start us, length us, event | category | flops | bytes accessed | tf_op | source)
XLA Modules:
  0.0 14.2 jit_solution(7281687300415957795)
XLA Ops:
  0.6 12.8 %shard_map.101 = (bf16[2,16,128]{2,1,0:T(8,128)(2,1)S(1)}, f32[128,512]{1,0:T(8,128)S(1)}, f32[128,128]{1,0:T(8,128)S(1)}, f32[4,128]{1,0:T(4,128)S(1)}, f32[1,128]{1,0:T(1,128)S(1)}) custom-call(bf16[32,128]{1,0:T(8,128)(2,1)} %bitcast.6, bf16[32,128]{1,0:T(8,128)(2,1)} %bitcast.7, bf16[128,512]{1,0:T(8,128)(2,1)} %w_qkvg_hbm.1, ...), custom_call_target="tpu_custom_call" | custom-call | tf_op jit(solution)/shard_map/pallas_call | solution.py:416
  13.4 0.8 %shard_map.102 = (bf16[2,16,128]{2,1,0:T(8,128)(2,1)}, f32[128,512]{1,0:T(8,128)}, f32[128,128]{1,0:T(8,128)}, f32[4,128]{1,0:T(4,128)}, f32[1,128]{1,0:T(1,128)}) custom-call(bf16[2,16,128]{2,1,0:T(8,128)(2,1)S(1)} %get-tuple-element.15.refs_0_, f32[128,512]{1,0:T(8,128)S(1)} %get-tuple-element.16.refs_1_, f32[128,128]{1,0:T(8,128)S(1)} %get-tuple-element.17.refs_2_, ...), custom_call_target="tpu_custom_call" | custom-call | tf_op jit(solution)/shard_map/pallas_call | solution.py:439

commit v8 on v6

--- a/solution.py
+++ b/solution.py
@@ -133,6 +133,7 @@
 
 
 BLOCK = 128
+PIECE = 32
 VMEM_LIMIT = 16 * 1024 * 1024
 MASKED = -1e30
 BF16 = jnp.bfloat16
@@ -381,9 +382,16 @@
 
 
 def deliver(count, *refs):
+    pieces = []
+    for index in range(count):
+        rows = refs[index].shape[0]
+        step = min(rows, PIECE)
+        pieces += [(index, pl.ds(start, step)) for start in range(0, rows, step)]
     copies = [
-        pltpu.make_async_copy(refs[index], refs[count + index], refs[-1].at[index])
-        for index in range(count)
+        pltpu.make_async_copy(
+            refs[index].at[rows], refs[count + index].at[rows], refs[-1].at[piece]
+        )
+        for piece, (index, rows) in enumerate(pieces)
     ]
     for copy in copies:
         copy.start()
@@ -436,12 +444,13 @@
             collective_id=0, has_side_effects=True, vmem_limit_bytes=VMEM_LIMIT
         ),
     )(*[pltpu.with_memory_space_constraint(value, pltpu.HBM) for value in operands])
+    pieces = sum(-(-shape.shape[0] // PIECE) for shape in shapes)
     results = pl.pallas_call(
         functools.partial(deliver, len(shapes)),
         out_shape=shapes,
         in_specs=[vmem] * len(shapes),
         out_specs=[hbm] * len(shapes),
-        scratch_shapes=[pltpu.SemaphoreType.DMA((len(shapes),))],
+        scratch_shapes=[pltpu.SemaphoreType.DMA((pieces,))],
         compiler_params=pltpu.CompilerParams(vmem_limit_bytes=VMEM_LIMIT),
     )(*results)
     d_pair, d_qkvg, d_wout, d_wbias, d_gain = results

time: 13.7 us -> 13.7 us (level)
  no operation moved by 1% of the time
where the time goes in v8:
time: 13.7 us; the launch traced here: 13.5 us
  Pallas kernels  12.9 us (94%)
  between operations  0.64 us (5%)
    pallas_call x1, Pallas kernels, gathered_plan(): pl.pallas_call(functools.partial(whole_crop, n, local), out_shape=[pltpu....  12.1 us
    pallas_call x1, Pallas kernels, gathered_plan(): pl.pallas_call(functools.partial(deliver, len(shapes)), out_shape=shapes,...  0.81 us

profile of v8, /device:TPU:0, one launch (start us, length us, event | category | flops | bytes accessed | tf_op | source)
XLA Modules:
  0.0 13.5 jit_solution(16863643027008347280)
XLA Ops:
  0.6 12.1 %shard_map.101 = (bf16[2,16,128]{2,1,0:T(8,128)(2,1)S(1)}, f32[128,512]{1,0:T(8,128)S(1)}, f32[128,128]{1,0:T(8,128)S(1)}, f32[4,128]{1,0:T(4,128)S(1)}, f32[1,128]{1,0:T(1,128)S(1)}) custom-call(bf16[32,128]{1,0:T(8,128)(2,1)} %bitcast.6, bf16[32,128]{1,0:T(8,128)(2,1)} %bitcast.7, bf16[128,512]{1,0:T(8,128)(2,1)} %w_qkvg_hbm.1, ...), custom_call_target="tpu_custom_call" | custom-call | tf_op jit(solution)/shard_map/pallas_call | solution.py:424
  12.7 0.8 %shard_map.102 = (bf16[2,16,128]{2,1,0:T(8,128)(2,1)}, f32[128,512]{1,0:T(8,128)}, f32[128,128]{1,0:T(8,128)}, f32[4,128]{1,0:T(4,128)}, f32[1,128]{1,0:T(1,128)}) custom-call(bf16[2,16,128]{2,1,0:T(8,128)(2,1)S(1)} %get-tuple-element.15.refs_0_, f32[128,512]{1,0:T(8,128)S(1)} %get-tuple-element.16.refs_1_, f32[128,128]{1,0:T(8,128)S(1)} %get-tuple-element.17.refs_2_, ...), custom_call_target="tpu_custom_call" | custom-call | tf_op jit(solution)/shard_map/pallas_call | solution.py:448
